TPU v7x, 512 devices: a whole 4x8x8 slice. The times are simulated.
512 devices in a mesh: loop: 16 (over y, x_hi), dp: 32 (over z, x_lo, core).
Axes of the slice: x: 4 (x_hi: 2, x_lo: 2; x = x_hi * 2 + x_lo), y: 8, z: 8, core: 2. Of those that a mesh axis runs over, the one named last changes fastest.
Arguments:
- images: bfloat16 [32, 32, 16, 16, 768], P('dp', 'loop'), may hold values from -6 to 6
- kernel: float32 [7, 7, 768], replicated, may hold values from -0.875 to 0.875
- ln_gain: float32 [768], replicated, may hold values from 0.5 to 1.5
- w_up: bfloat16 [768, 1536], P('dp'), may hold values from -0.21875 to 0.21875
- b_up: float32 [1536], replicated, may hold values from -3 to 3
- w_down: bfloat16 [1536, 768], P('dp'), may hold values from -0.15625 to 0.15625
- layer_scale: float32 [768], replicated, may hold values from 0.3 to 1
- w_head: bfloat16 [768, 1152], P('dp'), may hold values from -0.21875 to 0.21875
- text_rows: bfloat16 [32, 32, 1152], P('dp', 'loop'), may hold values from -6 to 6
- pair_ids: int32 [32, 32], P('dp', 'loop'), may hold values from 0 to 31, each once within a row
- log_temp: float32 [1], replicated, may hold values from 1.5 to 2.5
- loss_bias: float32 [1], replicated, may hold values from -6 to -2
Outputs:
- kernel_grad: float32 [7, 7, 768], replicated
- up_grad: float32 [768, 1536], P('dp')
- text_grad: float32 [32, 32, 1152], P('dp', 'loop')
Inputs may be any that keep to these rules, and one draw needn't show every extreme that they name: Each row of pair_ids holds every index of its group once.
All inputs are finite; a program needn't handle non-finite values.
Results may differ from a plain program's by a relative error of at most 0.04.
Values may be sent and summed in bfloat16 or wider, within the bound.
A program may use at most 64 MiB of HBM per device.

v0:
```python
import jax
import jax.numpy as jnp
from jax import lax
from jax.sharding import PartitionSpec as P

epsilon = 1e-06


def passed_along(value, axis, steps):
    count = lax.axis_size(axis)
    pairs = [(source, (source + steps) % count) for source in range(count)]
    return lax.ppermute(value, axis, pairs)


def image_tower(kernel, w_up, images, ln_gain, b_up, w_down, layer_scale, w_head):
    image_count = images.shape[0]
    grid_side = images.shape[1]
    channels = images.shape[3]
    padded = jnp.pad(images, ((0, 0), (3, 3), (3, 3), (0, 0)))
    conv_out = jnp.zeros(images.shape, jnp.float32)
    for row_off in range(7):
        for col_off in range(7):
            window = padded[:, row_off : row_off + grid_side, col_off : col_off + grid_side, :]
            conv_out = conv_out + window.astype(jnp.float32) * kernel[row_off, col_off]
    chan_mean = jnp.mean(conv_out, axis=-1, keepdims=True)
    centered = conv_out - chan_mean
    chan_var = jnp.mean(centered * centered, axis=-1, keepdims=True)
    normed = (centered * lax.rsqrt(chan_var + epsilon) * ln_gain).astype(jnp.bfloat16)
    flat_rows = normed.reshape(-1, channels)
    hidden = jnp.dot(flat_rows, w_up, preferred_element_type=jnp.float32) + b_up
    active = jax.nn.gelu(hidden, approximate=True).astype(jnp.bfloat16)
    mlp_out = jnp.dot(active, w_down, preferred_element_type=jnp.float32)
    block_out = images.reshape(-1, channels).astype(jnp.float32) + layer_scale * mlp_out
    pooled = jnp.mean(
        block_out.reshape(image_count, grid_side * grid_side, channels), axis=1
    ).astype(jnp.bfloat16)
    embedding = jnp.dot(pooled, w_head, preferred_element_type=jnp.float32)
    return embedding * lax.rsqrt(jnp.sum(embedding * embedding, axis=-1, keepdims=True) + epsilon)


def pair_grad(image_emb, text_emb, pair_row, text_index, logit_scale, logit_bias, group_size):
    logits = (
        logit_scale * jnp.dot(image_emb, text_emb.T, precision=lax.Precision.HIGHEST) + logit_bias
    )
    sign_of = jnp.where(pair_row[:, None] == text_index[None, :], 1.0, -1.0)
    return -sign_of * jax.nn.sigmoid(-sign_of * logits) / group_size


def body(
    images,
    kernel,
    ln_gain,
    w_up,
    b_up,
    w_down,
    layer_scale,
    w_head,
    text_rows,
    pair_ids,
    log_temp,
    loss_bias,
):
    loop_size = lax.axis_size("loop")
    loop_index = lax.axis_index("loop")
    up_full, down_full, head_full = (
        lax.all_gather(w_up, "dp", axis=0, tiled=True),
        lax.all_gather(w_down, "dp", axis=0, tiled=True),
        lax.all_gather(w_head, "dp", axis=0, tiled=True),
    )
    pictures = images[0]
    pair_row = pair_ids[0]
    img_dev = pictures.shape[0]
    group_size = img_dev * loop_size
    logit_scale = jnp.exp(log_temp[0])
    logit_bias = loss_bias[0]

    def run_tower(kernel_arg, up_arg):
        return image_tower(
            kernel_arg, up_arg, pictures, ln_gain, b_up, down_full, layer_scale, head_full
        )

    image_emb, pullback = jax.vjp(run_tower, kernel, up_full)
    raw_rows = text_rows[0].astype(jnp.float32)
    text_norm = jnp.sqrt(jnp.sum(raw_rows * raw_rows, axis=-1, keepdims=True) + epsilon)
    text_hat = raw_rows / text_norm
    rounded = lax.optimization_barrier(text_hat.astype(jnp.bfloat16))
    local_index = jnp.arange(img_dev, dtype=jnp.int32)

    def cycle_step(step_index, state):
        text_block, partials, image_cot = state
        source = (loop_index - step_index) % loop_size
        text_index = source * img_dev + local_index
        pair_weight = pair_grad(
            image_emb, text_block, pair_row, text_index, logit_scale, logit_bias, group_size
        )
        image_cot = image_cot + logit_scale * jnp.dot(
            pair_weight, text_block, precision=lax.Precision.HIGHEST
        )
        partials = partials + logit_scale * jnp.dot(
            pair_weight.T, image_emb, precision=lax.Precision.HIGHEST
        )
        text_block, partials = passed_along((text_block, partials), "loop", 1)
        return (text_block, partials, image_cot)

    start = (
        rounded.astype(jnp.float32),
        jnp.zeros(raw_rows.shape, jnp.float32),
        jnp.zeros(image_emb.shape, jnp.float32),
    )
    _, text_cot, image_cot = lax.fori_loop(0, loop_size, cycle_step, start)
    text_grad = (
        text_cot - text_hat * jnp.sum(text_hat * text_cot, axis=-1, keepdims=True)
    ) / text_norm
    kernel_part, up_part = pullback(image_cot)
    kernel_grad = lax.psum(kernel_part, ("loop", "dp"))
    up_rows = lax.psum_scatter(
        up_part.astype(jnp.float32).astype(jnp.bfloat16), "dp", scatter_dimension=0, tiled=True
    )
    up_grad = lax.psum(up_rows, "loop").astype(jnp.float32)
    return (kernel_grad, up_grad, text_grad[None])


def solution(mesh):
    placed = (
        P("dp", "loop", None, None, None),
        P(),
        P(),
        P("dp", None),
        P(),
        P("dp", None),
        P(),
        P("dp", None),
        P("dp", "loop", None),
        P("dp", "loop"),
        P(),
        P(),
    )
    return jax.shard_map(
        body,
        mesh=mesh,
        in_specs=placed,
        out_specs=(P(), P("dp", None), P("dp", "loop", None)),
        check_vma=False,
    )
```

profile of v0, /device:TPU:1, one launch (start us, length us, event | category | flops | bytes accessed | tf_op | source)
XLA Modules:
  0.0 996.5 jit_solution(3485320233537033907)
XLA Ops:
  15.5 30.5 %fusion.140 = (f32[2,16,16]{2,1,0:T(8,128)S(1)}, f32[2,16,16,768]{3,2,1,0:T(8,128)S(1)}) fusion(f32[768]{0:T(1024)S(1)} %get-tuple-element.377, f32[768]{0:T(1024)S(1)} %get-tuple-element.378, f32[768]{0:T(1024)S(1)} %get-tuple-element.331, f32[768]{0:T(1024)S(1)} %get-tuple-element.332, f32[768]{0:T(1024)S(1)} %get-tuple-element.333, ...), kind=kLoop, calls=%fused_computation.374 | loop fusion | flops 57802240 | bytes 2511872 | tf_op jit(solution)/shard_map/jvp()/reduce_sum | solution.py:25
  46.7 37.7 %all-gather.4.cloned.1.call-done = bf16[768,1536]{1,0:T(8,128)(2,1)} async-done(((bf16[24,1536]{1,0:T(8,128)(2,1)}), bf16[768,1536]{1,0:T(8,128)(2,1)}) %all-gather.4.cloned.1.call-update) | async-done | bytes 2359312 | tf_op jit(solution)/shard_map/all_gather | solution.py:66
  84.4 4.8 convolution_add_fusion
  89.2 65.1 %all-gather.6.cloned.1.call-done = bf16[1536,768]{1,0:T(8,128)(2,1)} async-done(((bf16[48,768]{1,0:T(8,128)(2,1)}), bf16[1536,768]{1,0:T(8,128)(2,1)}) %all-gather.6.cloned.1.call-update) | async-done | bytes 2359312 | tf_op jit(solution)/shard_map/all_gather | solution.py:67
  154.3 4.6 bitcast_reduce_fusion
  158.9 64.5 %all-gather.8.cloned.1.call-done = bf16[768,1152]{1,0:T(8,128)(2,1)} async-done(((bf16[24,1152]{1,0:T(8,128)(2,1)}), bf16[768,1152]{1,0:T(8,128)(2,1)}) %all-gather.8.cloned.1.call-update) | async-done | bytes 1769488 | tf_op jit(solution)/shard_map/all_gather | solution.py:68
  225.4 184.7 %while.20 = (s32[]{:T(128)}, f32[2,1152]{1,0:T(2,128)S(1)}, f32[2,1152]{1,0:T(2,128)S(1)}, f32[2,1152]{1,0:T(2,128)S(1)}, f32[]{:T(128)}, /*index=5*/s32[1,2]{1,...) while((s32[]{:T(128)}, f32[2,1152]{1,0:T(2,128)S(1)}, ...), condition=%wide.region_6.7_spmd.clone, body=%wide.region_5.6_spmd.clone.sunk | while | flops 177470 | bytes 166336 | solution.py:110
  225.5 4.3 collective-permute-start
  230.9 3.4 collective-permute-start.1
  234.5 4.4 collective-permute-done.1
  242.0 4.6 collective-permute-start.1
  246.8 3.2 collective-permute-done.1
  253.7 3.4 collective-permute-start.1
  257.3 4.4 collective-permute-done.1
  264.8 4.6 collective-permute-start.1
  269.5 3.2 collective-permute-done.1
  276.4 3.4 collective-permute-start.1
  280.0 4.4 collective-permute-done.1
  287.5 4.6 collective-permute-start.1
  292.3 3.2 collective-permute-done.1
  299.1 5.2 collective-permute-start.1
  307.1 3.1 collective-permute-start
  311.4 6.0 collective-permute-start.1
  319.4 3.9 collective-permute-start
  324.4 3.9 collective-permute-start.1
  328.5 4.0 collective-permute-done.1
  335.6 3.8 collective-permute-start.1
  339.6 4.1 collective-permute-done.1
  346.7 3.8 collective-permute-start.1
  350.7 4.1 collective-permute-done.1
  357.8 3.8 collective-permute-start.1
  361.8 4.1 collective-permute-done.1
  368.9 3.8 collective-permute-start.1
  372.8 4.1 collective-permute-done.1
  380.0 3.8 collective-permute-start.1
  384.0 4.0 collective-permute-done.1
  391.1 3.8 collective-permute-start.1
  395.0 4.1 collective-permute-done.1
  402.2 4.1 collective-permute-start.1
  406.5 3.7 collective-permute-done.1
  412.6 4.6 fusion.14
  421.3 3.6 fusion.143
  426.0 5.0 fusion.117
  431.1 3.7 fusion.23
  434.9 3.9 fusion.118
  440.1 119.1 %reduce-scatter.2.cloned.1.call-done = bf16[24,1536]{1,0:T(8,128)(2,1)} async-done(((bf16[768,1536]{1,0:T(8,128)(2,1)}), bf16[24,1536]{1,0:T(8,128)(2,1)}) %reduce-scatter.2.cloned.1.call-update) | async-done | bytes 73744 | tf_op jit(solution)/shard_map/reduce_scatter | solution.py:116
  560.5 148.9 %all-reduce.55.cloned.1.call-done = bf16[24,1536]{1,0:T(8,128)(2,1)} async-done(((bf16[24,1536]{1,0:T(8,128)(2,1)}), bf16[24,1536]{1,0:T(8,128)(2,1)}) %all-reduce.55.cloned.1.call-update) | async-done | bytes 73744 | tf_op jit(solution)/shard_map/psum | solution.py:119
  711.0 277.1 %all-reduce.53.cloned.1.call-done = f32[7,7,768]{2,1,0:T(8,128)} async-done(((f32[7,7,768]{2,1,0:T(8,128)}), f32[7,7,768]{2,1,0:T(8,128)}) %all-reduce.53.cloned.1.call-update) | async-done | bytes 150544 | tf_op jit(solution)/shard_map/psum | solution.py:115
  (216 shorter events, 74.9 us)
Async XLA Ops:
  7.2 77.2 %all-gather.4.cloned.1.call-start = ((), (), s32[]{:S(2)}) async-start(), calls=%async_computation.1 | async-start | bytes 2433024 | tf_op jit(solution)/shard_map/all_gather | solution.py:66
  7.9 146.4 %all-gather.6.cloned.1.call-start = ((), (), s32[]{:S(2)}) async-start(), calls=%async_computation.2 | async-start | bytes 2433024 | tf_op jit(solution)/shard_map/all_gather | solution.py:67
  8.6 214.8 %all-gather.8.cloned.1.call-start = ((), (), s32[]{:S(2)}) async-start(), calls=%async_computation.3 | async-start | bytes 1824768 | tf_op jit(solution)/shard_map/all_gather | solution.py:68
  9.4 549.9 %reduce-scatter.2.cloned.1.call-start = ((), (), s32[]{:S(2)}) async-start(), calls=%async_computation.5 | async-start | bytes 2433024 | tf_op jit(solution)/shard_map/reduce_scatter | solution.py:116
  15.5 30.9 %copy-start.1 = (f32[768]{0:T(1024)S(1)}, f32[768]{0:T(1024)}, u32[]{:S(2)}) copy-start(f32[768]{0:T(1024)} %param.16) | copy-start | bytes 9220
  46.4 38.0 %copy-start.4 = (f32[1536]{0:T(1024)S(1)}, f32[1536]{0:T(1024)}, u32[]{:S(2)}) copy-start(f32[1536]{0:T(1024)} %param.18) | copy-start | bytes 18436
  84.4 69.9 %copy-start = (bf16[1,2,16,16,768]{4,3,2,1,0:T(8,128)(2,1)S(1)}, bf16[1,2,16,16,768]{4,3,2,1,0:T(8,128)(2,1)}, u32[]{:S(2)}) copy-start(bf16[1,2,16,16,768]{4,3,2,1,0:T(8,128)(2,1)} %param.14) | copy-start | bytes 2359300
  84.4 69.9 %copy-start.2 = (f32[768]{0:T(1024)S(1)}, f32[768]{0:T(1024)}, u32[]{:S(2)}) copy-start(f32[768]{0:T(1024)} %param.20) | copy-start | bytes 9220
  158.9 66.5 %copy-start.5 = (s32[1,2]{1,0:T(1,128)S(1)}, s32[1,2]{1,0:T(1,128)}, u32[]{:S(2)}) copy-start(s32[1,2]{1,0:T(1,128)} %param.23) | copy-start | bytes 28
  225.5 13.5 %collective-permute-start = (f32[2,1152]{1,0:T(2,128)S(1)}, f32[2,1152]{1,0:T(2,128)S(1)}, u32[]{:S(2)}, u32[]{:S(2)}) collective-permute-start(f32[2,1152]{1,0:T(2,128)S(1)} %copy.20), channel_id=1, source_target_pairs={{0,32},{32,64},{64,96},{96,128},{128,160},{160,192},{192,224},{224... | collective-permute-start | bytes 27656 | tf_op jit(solution)/shard_map/while/body/eval_jaxpr/ppermute | solution.py:12
  230.9 8.0 collective-permute-start.1
  239.0 11.1 %collective-permute-start = (f32[2,1152]{1,0:T(2,128)S(1)}, f32[2,1152]{1,0:T(2,128)S(1)}, u32[]{:S(2)}, u32[]{:S(2)}) collective-permute-start(f32[2,1152]{1,0:T(2,128)S(1)} %copy.20), channel_id=1, source_target_pairs={{0,32},{32,64},{64,96},{96,128},{128,160},{160,192},{192,224},{224... | collective-permute-start | bytes 27656 | tf_op jit(solution)/shard_map/while/body/eval_jaxpr/ppermute | solution.py:12
  242.0 8.0 collective-permute-start.1
  250.1 11.6 %collective-permute-start = (f32[2,1152]{1,0:T(2,128)S(1)}, f32[2,1152]{1,0:T(2,128)S(1)}, u32[]{:S(2)}, u32[]{:S(2)}) collective-permute-start(f32[2,1152]{1,0:T(2,128)S(1)} %copy.20), channel_id=1, source_target_pairs={{0,32},{32,64},{64,96},{96,128},{128,160},{160,192},{192,224},{224... | collective-permute-start | bytes 27656 | tf_op jit(solution)/shard_map/while/body/eval_jaxpr/ppermute | solution.py:12
  253.7 8.0 collective-permute-start.1
  261.7 11.1 %collective-permute-start = (f32[2,1152]{1,0:T(2,128)S(1)}, f32[2,1152]{1,0:T(2,128)S(1)}, u32[]{:S(2)}, u32[]{:S(2)}) collective-permute-start(f32[2,1152]{1,0:T(2,128)S(1)} %copy.20), channel_id=1, source_target_pairs={{0,32},{32,64},{64,96},{96,128},{128,160},{160,192},{192,224},{224... | collective-permute-start | bytes 27656 | tf_op jit(solution)/shard_map/while/body/eval_jaxpr/ppermute | solution.py:12
  264.8 8.0 collective-permute-start.1
  272.8 11.6 %collective-permute-start = (f32[2,1152]{1,0:T(2,128)S(1)}, f32[2,1152]{1,0:T(2,128)S(1)}, u32[]{:S(2)}, u32[]{:S(2)}) collective-permute-start(f32[2,1152]{1,0:T(2,128)S(1)} %copy.20), channel_id=1, source_target_pairs={{0,32},{32,64},{64,96},{96,128},{128,160},{160,192},{192,224},{224... | collective-permute-start | bytes 27656 | tf_op jit(solution)/shard_map/while/body/eval_jaxpr/ppermute | solution.py:12
  276.4 8.0 collective-permute-start.1
  284.4 11.1 %collective-permute-start = (f32[2,1152]{1,0:T(2,128)S(1)}, f32[2,1152]{1,0:T(2,128)S(1)}, u32[]{:S(2)}, u32[]{:S(2)}) collective-permute-start(f32[2,1152]{1,0:T(2,128)S(1)} %copy.20), channel_id=1, source_target_pairs={{0,32},{32,64},{64,96},{96,128},{128,160},{160,192},{192,224},{224... | collective-permute-start | bytes 27656 | tf_op jit(solution)/shard_map/while/body/eval_jaxpr/ppermute | solution.py:12
  287.5 8.0 collective-permute-start.1
  295.5 11.6 %collective-permute-start = (f32[2,1152]{1,0:T(2,128)S(1)}, f32[2,1152]{1,0:T(2,128)S(1)}, u32[]{:S(2)}, u32[]{:S(2)}) collective-permute-start(f32[2,1152]{1,0:T(2,128)S(1)} %copy.20), channel_id=1, source_target_pairs={{0,32},{32,64},{64,96},{96,128},{128,160},{160,192},{192,224},{224... | collective-permute-start | bytes 27656 | tf_op jit(solution)/shard_map/while/body/eval_jaxpr/ppermute | solution.py:12
  299.1 8.0 collective-permute-start.1
  307.1 12.3 %collective-permute-start = (f32[2,1152]{1,0:T(2,128)S(1)}, f32[2,1152]{1,0:T(2,128)S(1)}, u32[]{:S(2)}, u32[]{:S(2)}) collective-permute-start(f32[2,1152]{1,0:T(2,128)S(1)} %copy.20), channel_id=1, source_target_pairs={{0,32},{32,64},{64,96},{96,128},{128,160},{160,192},{192,224},{224... | collective-permute-start | bytes 27656 | tf_op jit(solution)/shard_map/while/body/eval_jaxpr/ppermute | solution.py:12
  311.4 8.0 collective-permute-start.1
  319.4 13.1 %collective-permute-start = (f32[2,1152]{1,0:T(2,128)S(1)}, f32[2,1152]{1,0:T(2,128)S(1)}, u32[]{:S(2)}, u32[]{:S(2)}) collective-permute-start(f32[2,1152]{1,0:T(2,128)S(1)} %copy.20), channel_id=1, source_target_pairs={{0,32},{32,64},{64,96},{96,128},{128,160},{160,192},{192,224},{224... | collective-permute-start | bytes 27656 | tf_op jit(solution)/shard_map/while/body/eval_jaxpr/ppermute | solution.py:12
  324.4 8.0 collective-permute-start.1
  332.5 11.2 %collective-permute-start = (f32[2,1152]{1,0:T(2,128)S(1)}, f32[2,1152]{1,0:T(2,128)S(1)}, u32[]{:S(2)}, u32[]{:S(2)}) collective-permute-start(f32[2,1152]{1,0:T(2,128)S(1)} %copy.20), channel_id=1, source_target_pairs={{0,32},{32,64},{64,96},{96,128},{128,160},{160,192},{192,224},{224... | collective-permute-start | bytes 27656 | tf_op jit(solution)/shard_map/while/body/eval_jaxpr/ppermute | solution.py:12
  335.6 8.0 collective-permute-start.1
  343.7 11.1 %collective-permute-start = (f32[2,1152]{1,0:T(2,128)S(1)}, f32[2,1152]{1,0:T(2,128)S(1)}, u32[]{:S(2)}, u32[]{:S(2)}) collective-permute-start(f32[2,1152]{1,0:T(2,128)S(1)} %copy.20), channel_id=1, source_target_pairs={{0,32},{32,64},{64,96},{96,128},{128,160},{160,192},{192,224},{224... | collective-permute-start | bytes 27656 | tf_op jit(solution)/shard_map/while/body/eval_jaxpr/ppermute | solution.py:12
  346.7 8.0 collective-permute-start.1
  354.7 11.1 %collective-permute-start = (f32[2,1152]{1,0:T(2,128)S(1)}, f32[2,1152]{1,0:T(2,128)S(1)}, u32[]{:S(2)}, u32[]{:S(2)}) collective-permute-start(f32[2,1152]{1,0:T(2,128)S(1)} %copy.20), channel_id=1, source_target_pairs={{0,32},{32,64},{64,96},{96,128},{128,160},{160,192},{192,224},{224... | collective-permute-start | bytes 27656 | tf_op jit(solution)/shard_map/while/body/eval_jaxpr/ppermute | solution.py:12
  357.8 8.0 collective-permute-start.1
  365.8 11.1 %collective-permute-start = (f32[2,1152]{1,0:T(2,128)S(1)}, f32[2,1152]{1,0:T(2,128)S(1)}, u32[]{:S(2)}, u32[]{:S(2)}) collective-permute-start(f32[2,1152]{1,0:T(2,128)S(1)} %copy.20), channel_id=1, source_target_pairs={{0,32},{32,64},{64,96},{96,128},{128,160},{160,192},{192,224},{224... | collective-permute-start | bytes 27656 | tf_op jit(solution)/shard_map/while/body/eval_jaxpr/ppermute | solution.py:12
  368.9 8.0 collective-permute-start.1
  376.9 11.1 %collective-permute-start = (f32[2,1152]{1,0:T(2,128)S(1)}, f32[2,1152]{1,0:T(2,128)S(1)}, u32[]{:S(2)}, u32[]{:S(2)}) collective-permute-start(f32[2,1152]{1,0:T(2,128)S(1)} %copy.20), channel_id=1, source_target_pairs={{0,32},{32,64},{64,96},{96,128},{128,160},{160,192},{192,224},{224... | collective-permute-start | bytes 27656 | tf_op jit(solution)/shard_map/while/body/eval_jaxpr/ppermute | solution.py:12
  380.0 8.0 collective-permute-start.1
  388.0 11.1 %collective-permute-start = (f32[2,1152]{1,0:T(2,128)S(1)}, f32[2,1152]{1,0:T(2,128)S(1)}, u32[]{:S(2)}, u32[]{:S(2)}) collective-permute-start(f32[2,1152]{1,0:T(2,128)S(1)} %copy.20), channel_id=1, source_target_pairs={{0,32},{32,64},{64,96},{96,128},{128,160},{160,192},{192,224},{224... | collective-permute-start | bytes 27656 | tf_op jit(solution)/shard_map/while/body/eval_jaxpr/ppermute | solution.py:12
  391.1 8.0 collective-permute-start.1
  399.1 11.1 %collective-permute-start = (f32[2,1152]{1,0:T(2,128)S(1)}, f32[2,1152]{1,0:T(2,128)S(1)}, u32[]{:S(2)}, u32[]{:S(2)}) collective-permute-start(f32[2,1152]{1,0:T(2,128)S(1)} %copy.20), channel_id=1, source_target_pairs={{0,32},{32,64},{64,96},{96,128},{128,160},{160,192},{192,224},{224... | collective-permute-start | bytes 27656 | tf_op jit(solution)/shard_map/while/body/eval_jaxpr/ppermute | solution.py:12
  402.2 8.0 collective-permute-start.1
  410.2 2.4 copy-start.3
  417.2 1.2 copy-start.6
  421.2 288.2 %all-reduce.55.cloned.1.call-start = ((), (), s32[]{:S(2)}) async-start(), calls=%async_computation.6 | async-start | bytes 147456 | tf_op jit(solution)/shard_map/psum | solution.py:119
  559.3 428.8 %all-reduce.53.cloned.1.call-start = ((), (), s32[]{:S(2)}) async-start(), calls=%async_computation.4 | async-start | bytes 344064 | tf_op jit(solution)/shard_map/psum | solution.py:115
Sparse Core Ops, SparseCore 0:
  10.1 74.2 all-gather.3
  86.5 67.7 all-gather.5
  156.5 66.9 all-gather.7
  421.4 137.8 reduce-scatter.1
  562.0 147.3 all-reduce.54
  715.6 272.4 all-reduce.52
where the time goes:
time: 998 us; the launch traced here: 997 us
  waiting for transfers between devices  774 us (78%)
  starting transfers between devices  104 us (10%)
  other arithmetic  50 us (5%)
  matrix products  44.9 us (4%)
  between operations  15.4 us (2%)
    psum x1, waiting for transfers between devices, body(): kernel_grad = lax.psum(kernel_part, ('loop', 'dp'))  277 us
    psum x1, waiting for transfers between devices, body(): up_grad = lax.psum(up_rows, 'loop').astype(jnp.float32)  149 us
    reduce_scatter x1, waiting for transfers between devices, body(): lax.psum_scatter(up_part.astype(jnp.float32).astype(jnp.bfloat16), 'dp',...  119 us
    ppermute x32, starting transfers between devices, passed_along(): return lax.ppermute(value, axis, pairs)  104 us
    all_gather x1, waiting for transfers between devices, body(): lax.all_gather(w_down, 'dp', axis=0, tiled=True)  65.1 us
    all_gather x1, waiting for transfers between devices, body(): lax.all_gather(w_head, 'dp', axis=0, tiled=True)  64.5 us
    ppermute x32, waiting for transfers between devices, passed_along(): return lax.ppermute(value, axis, pairs)  59.5 us
    all_gather x1, waiting for transfers between devices, body(): lax.all_gather(w_up, 'dp', axis=0, tiled=True)  37.7 us
  transfers between devices with their start and end apart: 38, of which 22 were waited for; matrix products, arithmetic and copies ran while one was open for 9% of the time, Pallas kernels for 0%

commit v1 on v0

--- a/solution.py
+++ b/solution.py
@@ -112,7 +112,8 @@
         text_cot - text_hat * jnp.sum(text_hat * text_cot, axis=-1, keepdims=True)
     ) / text_norm
     kernel_part, up_part = pullback(image_cot)
-    kernel_grad = lax.psum(kernel_part, ("loop", "dp"))
+    one_axis = lax.psum(kernel_part, "loop")
+    kernel_grad = lax.psum(one_axis, "dp")
     up_rows = lax.psum_scatter(
         up_part.astype(jnp.float32).astype(jnp.bfloat16), "dp", scatter_dimension=0, tiled=True
     )

time: 998 us -> 1110 us (1.11)
  waiting for transfers between devices: 774 us -> 881 us
    psum x1 -> x2, waiting for transfers between devices: 277 us -> 379 us  [the longest x1 224 us: body(): kernel_grad = lax.psum(one_axis, 'dp')]
  transfers between devices with their start and end apart: 38 -> 39, of which waited for: 22 -> 23; matrix products, arithmetic and copies ran while one was open for 9% -> 8% of each run, Pallas kernels for 0% -> 0%
where the time goes in v1:
time: 1110 us; the launch traced here: 1100 us
  waiting for transfers between devices  881 us (79%)
  starting transfers between devices  104 us (9%)
  other arithmetic  50.4 us (5%)
  matrix products  45 us (4%)
  between operations  15.4 us (1%)
    psum x1, waiting for transfers between devices, body(): kernel_grad = lax.psum(one_axis, 'dp')  224 us
    psum x1, waiting for transfers between devices, body(): up_grad = lax.psum(up_rows, 'loop').astype(jnp.float32)  155 us
    psum x1, waiting for transfers between devices, body(): one_axis = lax.psum(kernel_part, 'loop')  155 us
    reduce_scatter x1, waiting for transfers between devices, body(): lax.psum_scatter(up_part.astype(jnp.float32).astype(jnp.bfloat16), 'dp',...  119 us
    ppermute x32, starting transfers between devices, passed_along(): return lax.ppermute(value, axis, pairs)  104 us
    all_gather x1, waiting for transfers between devices, body(): lax.all_gather(w_down, 'dp', axis=0, tiled=True)  65.1 us
    all_gather x1, waiting for transfers between devices, body(): lax.all_gather(w_head, 'dp', axis=0, tiled=True)  64.5 us
    ppermute x32, waiting for transfers between devices, passed_along(): return lax.ppermute(value, axis, pairs)  59.3 us
  transfers between devices with their start and end apart: 39, of which 23 were waited for; matrix products, arithmetic and copies ran while one was open for 8% of the time, Pallas kernels for 0%

profile of v1, /device:TPU:1, one launch (start us, length us, event | category | flops | bytes accessed | tf_op | source)
XLA Modules:
  0.0 1103.9 jit_solution(13268672736187167131)
XLA Ops:
  15.5 30.9 %fusion.140 = (f32[2,16,16]{2,1,0:T(8,128)S(1)}, f32[2,16,16,768]{3,2,1,0:T(8,128)S(1)}) fusion(f32[768]{0:T(1024)S(1)} %get-tuple-element.377, f32[768]{0:T(1024)S(1)} %get-tuple-element.378, f32[768]{0:T(1024)S(1)} %get-tuple-element.331, f32[768]{0:T(1024)S(1)} %get-tuple-element.332, f32[768]{0:T(1024)S(1)} %get-tuple-element.333, ...), kind=kLoop, calls=%fused_computation.374 | loop fusion | flops 57802240 | bytes 2511872 | tf_op jit(solution)/shard_map/jvp()/reduce_sum | solution.py:25
  47.0 37.4 %all-gather.4.cloned.1.call-done = bf16[768,1536]{1,0:T(8,128)(2,1)} async-done(((bf16[24,1536]{1,0:T(8,128)(2,1)}), bf16[768,1536]{1,0:T(8,128)(2,1)}) %all-gather.4.cloned.1.call-update) | async-done | bytes 2359312 | tf_op jit(solution)/shard_map/all_gather | solution.py:66
  84.4 4.8 convolution_add_fusion
  89.2 65.1 %all-gather.6.cloned.1.call-done = bf16[1536,768]{1,0:T(8,128)(2,1)} async-done(((bf16[48,768]{1,0:T(8,128)(2,1)}), bf16[1536,768]{1,0:T(8,128)(2,1)}) %all-gather.6.cloned.1.call-update) | async-done | bytes 2359312 | tf_op jit(solution)/shard_map/all_gather | solution.py:67
  154.3 4.6 bitcast_reduce_fusion
  158.9 64.5 %all-gather.8.cloned.1.call-done = bf16[768,1152]{1,0:T(8,128)(2,1)} async-done(((bf16[24,1152]{1,0:T(8,128)(2,1)}), bf16[768,1152]{1,0:T(8,128)(2,1)}) %all-gather.8.cloned.1.call-update) | async-done | bytes 1769488 | tf_op jit(solution)/shard_map/all_gather | solution.py:68
  225.5 184.7 %while.20 = (s32[]{:T(128)}, f32[2,1152]{1,0:T(2,128)S(1)}, f32[2,1152]{1,0:T(2,128)S(1)}, f32[2,1152]{1,0:T(2,128)S(1)}, f32[]{:T(128)}, /*index=5*/s32[1,2]{1,...) while((s32[]{:T(128)}, f32[2,1152]{1,0:T(2,128)S(1)}, ...), condition=%wide.region_6.7_spmd.clone, body=%wide.region_5.6_spmd.clone.sunk | while | flops 177470 | bytes 166336 | solution.py:110
  225.5 4.3 collective-permute-start
  231.0 3.4 collective-permute-start.1
  234.6 4.4 collective-permute-done.1
  242.1 4.6 collective-permute-start.1
  246.8 3.2 collective-permute-done.1
  253.7 3.4 collective-permute-start.1
  257.3 4.4 collective-permute-done.1
  264.8 4.6 collective-permute-start.1
  269.6 3.2 collective-permute-done.1
  276.4 3.4 collective-permute-start.1
  280.0 4.4 collective-permute-done.1
  287.5 4.6 collective-permute-start.1
  292.3 3.2 collective-permute-done.1
  299.1 5.2 collective-permute-start.1
  311.4 6.0 collective-permute-start.1
  319.4 3.9 collective-permute-start
  324.5 3.9 collective-permute-start.1
  328.5 4.0 collective-permute-done.1
  335.6 3.8 collective-permute-start.1
  339.6 4.0 collective-permute-done.1
  346.7 3.8 collective-permute-start.1
  350.7 4.1 collective-permute-done.1
  357.8 3.8 collective-permute-start.1
  361.8 4.1 collective-permute-done.1
  368.9 3.8 collective-permute-start.1
  372.9 4.0 collective-permute-done.1
  380.0 3.8 collective-permute-start.1
  384.0 4.0 collective-permute-done.1
  391.1 3.8 collective-permute-start.1
  395.1 4.0 collective-permute-done.1
  402.2 4.1 collective-permute-start.1
  406.5 3.7 collective-permute-done.1
  412.6 4.6 fusion.14
  421.3 3.6 fusion.143
  426.0 5.0 fusion.117
  431.2 3.7 fusion.23
  434.9 3.9 fusion.118
  440.2 119.0 %reduce-scatter.2.cloned.1.call-done = bf16[24,1536]{1,0:T(8,128)(2,1)} async-done(((bf16[768,1536]{1,0:T(8,128)(2,1)}), bf16[24,1536]{1,0:T(8,128)(2,1)}) %reduce-scatter.2.cloned.1.call-update) | async-done | bytes 73744 | tf_op jit(solution)/shard_map/reduce_scatter | solution.py:117
  559.4 154.8 %all-reduce.54.cloned.1.call-done = f32[7,7,768]{2,1,0:T(8,128)} async-done(((f32[7,7,768]{2,1,0:T(8,128)}), f32[7,7,768]{2,1,0:T(8,128)}) %all-reduce.54.cloned.1.call-update) | async-done | bytes 150544 | tf_op jit(solution)/shard_map/psum | solution.py:115
  715.0 155.0 %all-reduce.58.cloned.1.call-done = bf16[24,1536]{1,0:T(8,128)(2,1)} async-done(((bf16[24,1536]{1,0:T(8,128)(2,1)}), bf16[24,1536]{1,0:T(8,128)(2,1)}) %all-reduce.58.cloned.1.call-update) | async-done | bytes 73744 | tf_op jit(solution)/shard_map/psum | solution.py:120
  871.6 223.9 %all-reduce.56.cloned.1.call-done = f32[7,7,768]{2,1,0:T(8,128)} async-done(((f32[7,7,768]{2,1,0:T(8,128)}), f32[7,7,768]{2,1,0:T(8,128)}) %all-reduce.56.cloned.1.call-update) | async-done | bytes 150544 | tf_op jit(solution)/shard_map/psum | solution.py:116
  (219 shorter events, 77.6 us)
Async XLA Ops:
  7.2 77.2 %all-gather.4.cloned.1.call-start = ((), (), s32[]{:S(2)}) async-start(), calls=%async_computation.1 | async-start | bytes 2433024 | tf_op jit(solution)/shard_map/all_gather | solution.py:66
  7.9 146.4 %all-gather.6.cloned.1.call-start = ((), (), s32[]{:S(2)}) async-start(), calls=%async_computation.2 | async-start | bytes 2433024 | tf_op jit(solution)/shard_map/all_gather | solution.py:67
  8.6 214.8 %all-gather.8.cloned.1.call-start = ((), (), s32[]{:S(2)}) async-start(), calls=%async_computation.3 | async-start | bytes 1824768 | tf_op jit(solution)/shard_map/all_gather | solution.py:68
  9.4 549.9 %reduce-scatter.2.cloned.1.call-start = ((), (), s32[]{:S(2)}) async-start(), calls=%async_computation.6 | async-start | bytes 2433024 | tf_op jit(solution)/shard_map/reduce_scatter | solution.py:117
  15.5 31.2 %copy-start.1 = (f32[768]{0:T(1024)S(1)}, f32[768]{0:T(1024)}, u32[]{:S(2)}) copy-start(f32[768]{0:T(1024)} %param.16) | copy-start | bytes 9220
  46.7 37.7 %copy-start.4 = (f32[1536]{0:T(1024)S(1)}, f32[1536]{0:T(1024)}, u32[]{:S(2)}) copy-start(f32[1536]{0:T(1024)} %param.18) | copy-start | bytes 18436
  84.4 69.9 %copy-start = (bf16[1,2,16,16,768]{4,3,2,1,0:T(8,128)(2,1)S(1)}, bf16[1,2,16,16,768]{4,3,2,1,0:T(8,128)(2,1)}, u32[]{:S(2)}) copy-start(bf16[1,2,16,16,768]{4,3,2,1,0:T(8,128)(2,1)} %param.14) | copy-start | bytes 2359300
  84.4 69.9 %copy-start.2 = (f32[768]{0:T(1024)S(1)}, f32[768]{0:T(1024)}, u32[]{:S(2)}) copy-start(f32[768]{0:T(1024)} %param.20) | copy-start | bytes 9220
  158.9 66.5 %copy-start.5 = (s32[1,2]{1,0:T(1,128)S(1)}, s32[1,2]{1,0:T(1,128)}, u32[]{:S(2)}) copy-start(s32[1,2]{1,0:T(1,128)} %param.23) | copy-start | bytes 28
  225.5 13.5 %collective-permute-start = (f32[2,1152]{1,0:T(2,128)S(1)}, f32[2,1152]{1,0:T(2,128)S(1)}, u32[]{:S(2)}, u32[]{:S(2)}) collective-permute-start(f32[2,1152]{1,0:T(2,128)S(1)} %copy.20), channel_id=1, source_target_pairs={{0,32},{32,64},{64,96},{96,128},{128,160},{160,192},{192,224},{224... | collective-permute-start | bytes 27656 | tf_op jit(solution)/shard_map/while/body/eval_jaxpr/ppermute | solution.py:12
  231.0 8.0 collective-permute-start.1
  239.0 11.1 %collective-permute-start = (f32[2,1152]{1,0:T(2,128)S(1)}, f32[2,1152]{1,0:T(2,128)S(1)}, u32[]{:S(2)}, u32[]{:S(2)}) collective-permute-start(f32[2,1152]{1,0:T(2,128)S(1)} %copy.20), channel_id=1, source_target_pairs={{0,32},{32,64},{64,96},{96,128},{128,160},{160,192},{192,224},{224... | collective-permute-start | bytes 27656 | tf_op jit(solution)/shard_map/while/body/eval_jaxpr/ppermute | solution.py:12
  242.1 8.0 collective-permute-start.1
  250.1 11.6 %collective-permute-start = (f32[2,1152]{1,0:T(2,128)S(1)}, f32[2,1152]{1,0:T(2,128)S(1)}, u32[]{:S(2)}, u32[]{:S(2)}) collective-permute-start(f32[2,1152]{1,0:T(2,128)S(1)} %copy.20), channel_id=1, source_target_pairs={{0,32},{32,64},{64,96},{96,128},{128,160},{160,192},{192,224},{224... | collective-permute-start | bytes 27656 | tf_op jit(solution)/shard_map/while/body/eval_jaxpr/ppermute | solution.py:12
  253.7 8.0 collective-permute-start.1
  261.7 11.1 %collective-permute-start = (f32[2,1152]{1,0:T(2,128)S(1)}, f32[2,1152]{1,0:T(2,128)S(1)}, u32[]{:S(2)}, u32[]{:S(2)}) collective-permute-start(f32[2,1152]{1,0:T(2,128)S(1)} %copy.20), channel_id=1, source_target_pairs={{0,32},{32,64},{64,96},{96,128},{128,160},{160,192},{192,224},{224... | collective-permute-start | bytes 27656 | tf_op jit(solution)/shard_map/while/body/eval_jaxpr/ppermute | solution.py:12
  264.8 8.0 collective-permute-start.1
  272.8 11.6 %collective-permute-start = (f32[2,1152]{1,0:T(2,128)S(1)}, f32[2,1152]{1,0:T(2,128)S(1)}, u32[]{:S(2)}, u32[]{:S(2)}) collective-permute-start(f32[2,1152]{1,0:T(2,128)S(1)} %copy.20), channel_id=1, source_target_pairs={{0,32},{32,64},{64,96},{96,128},{128,160},{160,192},{192,224},{224... | collective-permute-start | bytes 27656 | tf_op jit(solution)/shard_map/while/body/eval_jaxpr/ppermute | solution.py:12
  276.4 8.0 collective-permute-start.1
  284.4 11.1 %collective-permute-start = (f32[2,1152]{1,0:T(2,128)S(1)}, f32[2,1152]{1,0:T(2,128)S(1)}, u32[]{:S(2)}, u32[]{:S(2)}) collective-permute-start(f32[2,1152]{1,0:T(2,128)S(1)} %copy.20), channel_id=1, source_target_pairs={{0,32},{32,64},{64,96},{96,128},{128,160},{160,192},{192,224},{224... | collective-permute-start | bytes 27656 | tf_op jit(solution)/shard_map/while/body/eval_jaxpr/ppermute | solution.py:12
  287.5 8.0 collective-permute-start.1
  295.5 11.6 %collective-permute-start = (f32[2,1152]{1,0:T(2,128)S(1)}, f32[2,1152]{1,0:T(2,128)S(1)}, u32[]{:S(2)}, u32[]{:S(2)}) collective-permute-start(f32[2,1152]{1,0:T(2,128)S(1)} %copy.20), channel_id=1, source_target_pairs={{0,32},{32,64},{64,96},{96,128},{128,160},{160,192},{192,224},{224... | collective-permute-start | bytes 27656 | tf_op jit(solution)/shard_map/while/body/eval_jaxpr/ppermute | solution.py:12
  299.1 8.0 collective-permute-start.1
  307.2 12.2 %collective-permute-start = (f32[2,1152]{1,0:T(2,128)S(1)}, f32[2,1152]{1,0:T(2,128)S(1)}, u32[]{:S(2)}, u32[]{:S(2)}) collective-permute-start(f32[2,1152]{1,0:T(2,128)S(1)} %copy.20), channel_id=1, source_target_pairs={{0,32},{32,64},{64,96},{96,128},{128,160},{160,192},{192,224},{224... | collective-permute-start | bytes 27656 | tf_op jit(solution)/shard_map/while/body/eval_jaxpr/ppermute | solution.py:12
  311.4 8.0 collective-permute-start.1
  319.4 13.1 %collective-permute-start = (f32[2,1152]{1,0:T(2,128)S(1)}, f32[2,1152]{1,0:T(2,128)S(1)}, u32[]{:S(2)}, u32[]{:S(2)}) collective-permute-start(f32[2,1152]{1,0:T(2,128)S(1)} %copy.20), channel_id=1, source_target_pairs={{0,32},{32,64},{64,96},{96,128},{128,160},{160,192},{192,224},{224... | collective-permute-start | bytes 27656 | tf_op jit(solution)/shard_map/while/body/eval_jaxpr/ppermute | solution.py:12
  324.5 8.0 collective-permute-start.1
  332.5 11.2 %collective-permute-start = (f32[2,1152]{1,0:T(2,128)S(1)}, f32[2,1152]{1,0:T(2,128)S(1)}, u32[]{:S(2)}, u32[]{:S(2)}) collective-permute-start(f32[2,1152]{1,0:T(2,128)S(1)} %copy.20), channel_id=1, source_target_pairs={{0,32},{32,64},{64,96},{96,128},{128,160},{160,192},{192,224},{224... | collective-permute-start | bytes 27656 | tf_op jit(solution)/shard_map/while/body/eval_jaxpr/ppermute | solution.py:12
  335.6 8.0 collective-permute-start.1
  343.7 11.1 %collective-permute-start = (f32[2,1152]{1,0:T(2,128)S(1)}, f32[2,1152]{1,0:T(2,128)S(1)}, u32[]{:S(2)}, u32[]{:S(2)}) collective-permute-start(f32[2,1152]{1,0:T(2,128)S(1)} %copy.20), channel_id=1, source_target_pairs={{0,32},{32,64},{64,96},{96,128},{128,160},{160,192},{192,224},{224... | collective-permute-start | bytes 27656 | tf_op jit(solution)/shard_map/while/body/eval_jaxpr/ppermute | solution.py:12
  346.7 8.0 collective-permute-start.1
  354.8 11.1 %collective-permute-start = (f32[2,1152]{1,0:T(2,128)S(1)}, f32[2,1152]{1,0:T(2,128)S(1)}, u32[]{:S(2)}, u32[]{:S(2)}) collective-permute-start(f32[2,1152]{1,0:T(2,128)S(1)} %copy.20), channel_id=1, source_target_pairs={{0,32},{32,64},{64,96},{96,128},{128,160},{160,192},{192,224},{224... | collective-permute-start | bytes 27656 | tf_op jit(solution)/shard_map/while/body/eval_jaxpr/ppermute | solution.py:12
  357.8 8.0 collective-permute-start.1
  365.8 11.1 %collective-permute-start = (f32[2,1152]{1,0:T(2,128)S(1)}, f32[2,1152]{1,0:T(2,128)S(1)}, u32[]{:S(2)}, u32[]{:S(2)}) collective-permute-start(f32[2,1152]{1,0:T(2,128)S(1)} %copy.20), channel_id=1, source_target_pairs={{0,32},{32,64},{64,96},{96,128},{128,160},{160,192},{192,224},{224... | collective-permute-start | bytes 27656 | tf_op jit(solution)/shard_map/while/body/eval_jaxpr/ppermute | solution.py:12
  368.9 8.0 collective-permute-start.1
  376.9 11.1 %collective-permute-start = (f32[2,1152]{1,0:T(2,128)S(1)}, f32[2,1152]{1,0:T(2,128)S(1)}, u32[]{:S(2)}, u32[]{:S(2)}) collective-permute-start(f32[2,1152]{1,0:T(2,128)S(1)} %copy.20), channel_id=1, source_target_pairs={{0,32},{32,64},{64,96},{96,128},{128,160},{160,192},{192,224},{224... | collective-permute-start | bytes 27656 | tf_op jit(solution)/shard_map/while/body/eval_jaxpr/ppermute | solution.py:12
  380.0 8.0 collective-permute-start.1
  388.0 11.1 %collective-permute-start = (f32[2,1152]{1,0:T(2,128)S(1)}, f32[2,1152]{1,0:T(2,128)S(1)}, u32[]{:S(2)}, u32[]{:S(2)}) collective-permute-start(f32[2,1152]{1,0:T(2,128)S(1)} %copy.20), channel_id=1, source_target_pairs={{0,32},{32,64},{64,96},{96,128},{128,160},{160,192},{192,224},{224... | collective-permute-start | bytes 27656 | tf_op jit(solution)/shard_map/while/body/eval_jaxpr/ppermute | solution.py:12
  391.1 8.0 collective-permute-start.1
  399.1 11.1 %collective-permute-start = (f32[2,1152]{1,0:T(2,128)S(1)}, f32[2,1152]{1,0:T(2,128)S(1)}, u32[]{:S(2)}, u32[]{:S(2)}) collective-permute-start(f32[2,1152]{1,0:T(2,128)S(1)} %copy.20), channel_id=1, source_target_pairs={{0,32},{32,64},{64,96},{96,128},{128,160},{160,192},{192,224},{224... | collective-permute-start | bytes 27656 | tf_op jit(solution)/shard_map/while/body/eval_jaxpr/ppermute | solution.py:12
  402.2 8.0 collective-permute-start.1
  410.2 2.4 copy-start.3
  417.2 1.2 copy-start.6
  421.3 293.0 %all-reduce.54.cloned.1.call-start = ((), (), s32[]{:S(2)}) async-start(), calls=%async_computation.4 | async-start | bytes 344064 | tf_op jit(solution)/shard_map/psum | solution.py:115
  440.2 429.8 %all-reduce.58.cloned.1.call-start = ((), (), s32[]{:S(2)}) async-start(), calls=%async_computation.7 | async-start | bytes 147456 | tf_op jit(solution)/shard_map/psum | solution.py:120
  559.3 536.2 %all-reduce.56.cloned.1.call-start = ((), (), s32[]{:S(2)}) async-start(), calls=%async_computation.5 | async-start | bytes 344064 | tf_op jit(solution)/shard_map/psum | solution.py:116
Sparse Core Ops, SparseCore 0:
  10.1 74.2 all-gather.3
  86.5 67.7 all-gather.5
  156.5 66.9 all-gather.7
  421.4 137.7 reduce-scatter.1
  562.6 151.6 all-reduce.53
  717.3 152.6 all-reduce.57
  872.9 222.4 all-reduce.55
